TPU v7x, 32 devices: a whole 2x2x4 slice. The times are simulated.
32 devices in a mesh: row: 16 (over z, x, core), blk: 2 (over y).
Axes of the slice: x: 2, y: 2, z: 4, core: 2. Of those that a mesh axis runs over, the one named last changes fastest.
Arguments:
- factor_panel: bfloat16 [32768, 2, 2048], P('row', None, 'blk'), may hold values from -0.09375 to 0.09375
- right_side: float32 [256, 32768], P('blk', 'row'), may hold values from -6 to 6
- block_inverse: float32 [2, 2048, 2048], P(None, 'row', 'blk'), may hold values from -2 to 2, as said below
Outputs:
- solved: float32 [2, 256, 2048], P(None, 'blk', 'row')
- reduced_side: float32 [256, 32768], P('blk', 'row')
Inputs may be any that keep to these rules, and one draw needn't show every extreme that they name: block_inverse[k] is lower triangular with diagonal entries between 1 and 2.
All inputs are finite; a program needn't handle non-finite values.
Results may differ from a plain program's by a relative error of at most 0.015.
Values may be sent and summed in bfloat16 or wider, within the bound.
A program may use at most 64 MiB of HBM per device.

v0:
```python
import jax
import jax.numpy as jnp
from jax import lax
from jax.sharding import PartitionSpec as P

STEPS = 2


def from_root(array, axis, root):
    mine = lax.axis_index(axis) == root
    return lax.psum(jnp.where(mine, array, jnp.zeros_like(array)), axis)


def local(factor_panel, right_side, block_inverse):
    row_index = lax.axis_index("row")
    reduced_side = right_side
    outputs = []
    for section in range(STEPS):
        pivot_block = from_root(reduced_side, "row", section)
        pivot_cols = lax.all_to_all(pivot_block, "blk", split_axis=1, concat_axis=0, tiled=True)
        partial_value = jnp.dot(
            pivot_cols, block_inverse[section].T, precision=lax.Precision.HIGHEST
        )
        own_share = lax.psum_scatter(partial_value, "blk", scatter_dimension=0, tiled=True)
        gathered = lax.all_gather(own_share.astype(jnp.bfloat16), "row", axis=1, tiled=True)
        group_cols = lax.all_to_all(gathered, "blk", split_axis=1, concat_axis=0, tiled=True)
        outputs.append(own_share)
        panel_now = factor_panel[:, section, :]
        update = lax.psum_scatter(
            lax.dot_general(
                group_cols, panel_now, (((1,), (1,)), ((), ())), preferred_element_type=jnp.float32
            ).astype(jnp.bfloat16),
            "blk",
            scatter_dimension=0,
            tiled=True,
        ).astype(jnp.float32)
        reduced_side = reduced_side - jnp.where(row_index > section, update, jnp.float32(0.0))
    return (jnp.stack(outputs), reduced_side)


def solution(mesh):
    placed = (P("row", None, "blk"), P("blk", "row"), P(None, "row", "blk"))
    return jax.shard_map(
        local,
        mesh=mesh,
        in_specs=placed,
        out_specs=(P(None, "blk", "row"), P("blk", "row")),
        check_vma=False,
    )
```

profile of v0, /device:TPU:3, one launch (start us, length us, event | category | flops | bytes accessed | tf_op | source)
XLA Modules:
  0.0 395.5 jit_solution(17296178476216739360)
XLA Ops:
  7.2 0.0 all-reduce.3.cloned.1.call-start
  7.2 0.1 broadcast_select_fusion
  7.3 1.1 copy.30
  8.4 0.0 all-reduce.3.cloned.1.call-update
  8.4 0.0 reduce-scatter.5.cloned.1.call-start
  8.5 96.5 %all-reduce.3.cloned.1.call-done = f32[128,2,1024]{2,0,1:T(8,128)} async-done(((f32[128,2,1024]{2,0,1:T(8,128)}), f32[128,2,1024]{2,0,1:T(8,128)}) %all-reduce.3.cloned.1.call-update) | async-done | bytes 1048592 | tf_op jit(solution)/shard_map/psum | solution.py:11
  105.0 15.2 %all_to_all.76 = f32[128,2,1024]{2,0,1:T(8,128)S(1)} all-to-all(f32[128,2,1024]{2,0,1:T(8,128)} %all-reduce.3.cloned.1.call-done), channel_id=1, replica_groups=mesh['row'=16,'blk'=2] {'blk'}, dimensions={1} | all-to-all | bytes 2097152 | tf_op jit(solution)/shard_map/all_to_all | solution.py:20
  120.3 2.7 fusion.7
  122.9 0.0 reduce-scatter.5.cloned.1.call-update
  123.0 11.6 %reduce-scatter.5.cloned.1.call-done = f32[128,128]{1,0:T(8,128)} async-done(((f32[256,128]{1,0:T(8,128)}), f32[128,128]{1,0:T(8,128)}) %reduce-scatter.5.cloned.1.call-update) | async-done | bytes 65552 | tf_op jit(solution)/shard_map/reduce_scatter | solution.py:24
  134.5 0.8 convert_element_type.18
  135.4 19.7 %all_gather.6 = bf16[128,2048]{1,0:T(8,128)(2,1)S(1)} all-gather(bf16[128,128]{1,0:T(8,128)(2,1)S(1)} %convert_element_type.18), channel_id=1, replica_groups=mesh['row'=16,'blk'=2] {'row'}, dimensions={1}, use_global_device_ids=true | all-gather | bytes 557056 | tf_op jit(solution)/shard_map/all_gather | solution.py:25
  155.0 0.8 copy.32
  155.9 3.5 all-to-all-start.1
  159.4 0.0 reduce-scatter.7.cloned.1.call-start
  159.4 17.6 %fusion.11 = (bf16[2048,1,1024]{2,1,0:T(2,128)(2,1)}, bf16[2048,1,1024]{2,1,0:T(2,128)(2,1)}) fusion(bf16[2048,2,1024]{2,1,0:T(2,128)(2,1)} %param.3), kind=kLoop, calls=%fused_computation.21 | loop fusion | bytes 16777216 | tf_op jit(solution)/shard_map/slice | solution.py:28
  177.0 0.0 copy-start
  177.0 0.0 all-to-all-done.1
  177.0 0.0 copy-start.2
  177.0 6.1 %fusion.2 = bf16[256,2048]{1,0:T(8,128)(2,1)} fusion(bf16[256,1024]{1,0:T(8,128)(2,1)S(1)} %bitcast.59, bf16[2048,1,1024]{2,1,0:T(2,128)(2,1)} %get-tuple-element.3), kind=kOutput, calls=%fused_computation.4 | convolution fusion | flops 1074266112 | bytes 5767168 | tf_op jit(solution)/shard_map/dot_general | solution.py:30
  183.1 0.0 reduce-scatter.7.cloned.1.call-update
  183.2 0.0 all-reduce.5.cloned.1.call-start
  183.2 21.3 %reduce-scatter.7.cloned.1.call-done = bf16[128,2048]{1,0:T(8,128)(2,1)} async-done(((bf16[256,2048]{1,0:T(8,128)(2,1)}), bf16[128,2048]{1,0:T(8,128)(2,1)}) %reduce-scatter.7.cloned.1.call-update) | async-done | bytes 524304 | tf_op jit(solution)/shard_map/reduce_scatter | solution.py:29
  204.6 0.0 copy-done
  204.6 1.2 fusion.4
  205.8 1.0 copy.29
  206.8 0.0 copy-start.3
  206.8 0.0 copy-start.1
  206.8 0.0 all-reduce.5.cloned.1.call-update
  206.8 0.0 reduce-scatter.9.cloned.1.call-start
  206.9 93.5 %all-reduce.5.cloned.1.call-done = f32[128,2,1024]{2,0,1:T(8,128)} async-done(((f32[128,2,1024]{2,0,1:T(8,128)}), f32[128,2,1024]{2,0,1:T(8,128)}) %all-reduce.5.cloned.1.call-update) | async-done | bytes 1048592 | tf_op jit(solution)/shard_map/psum | solution.py:11
  300.4 15.2 %all_to_all.77 = f32[128,2,1024]{2,0,1:T(8,128)S(1)} all-to-all(f32[128,2,1024]{2,0,1:T(8,128)} %all-reduce.5.cloned.1.call-done), channel_id=1, replica_groups=mesh['row'=16,'blk'=2] {'blk'}, dimensions={1} | all-to-all | bytes 2097152 | tf_op jit(solution)/shard_map/all_to_all | solution.py:20
  315.7 0.0 copy-done.2
  315.7 1.6 fusion.5
  317.3 0.0 reduce-scatter.9.cloned.1.call-update
  317.3 0.0 reduce-scatter.11.cloned.1.call-start
  317.4 11.5 %reduce-scatter.9.cloned.1.call-done = f32[128,128]{1,0:T(8,128)} async-done(((f32[256,128]{1,0:T(8,128)}), f32[128,128]{1,0:T(8,128)}) %reduce-scatter.9.cloned.1.call-update) | async-done | bytes 65552 | tf_op jit(solution)/shard_map/reduce_scatter | solution.py:24
  328.9 0.9 convert_element_type.21
  329.8 19.7 %all_gather.7 = bf16[128,2048]{1,0:T(8,128)(2,1)S(1)} all-gather(bf16[128,128]{1,0:T(8,128)(2,1)S(1)} %convert_element_type.21), channel_id=1, replica_groups=mesh['row'=16,'blk'=2] {'row'}, dimensions={1}, use_global_device_ids=true | all-gather | bytes 557056 | tf_op jit(solution)/shard_map/all_gather | solution.py:25
  349.5 10.4 %all_to_all.78 = bf16[128,2,1024]{2,0,1:T(8,128)(2,1)S(1)} all-to-all(bf16[128,2,1024]{2,0,1:T(8,128)(2,1)S(1)} %bitcast.58), channel_id=1, replica_groups=mesh['row'=16,'blk'=2] {'blk'}, dimensions={1} | all-to-all | bytes 1048576 | tf_op jit(solution)/shard_map/all_to_all | solution.py:26
  359.9 5.9 %fusion.3 = bf16[256,2048]{1,0:T(8,128)(2,1)} fusion(bf16[256,1024]{1,0:T(8,128)(2,1)S(1)} %bitcast.60, bf16[2048,1,1024]{2,1,0:T(2,128)(2,1)} %get-tuple-element.2), kind=kOutput, calls=%fused_computation.5 | convolution fusion | flops 1074266112 | bytes 5767168 | tf_op jit(solution)/shard_map/dot_general | solution.py:30
  365.8 0.0 reduce-scatter.11.cloned.1.call-update
  365.9 0.0 copy-done.3
  365.9 0.0 copy-done.4
  365.9 0.7 pad_maximum_fusion
  366.6 19.9 %reduce-scatter.11.cloned.1.call-done = bf16[128,2048]{1,0:T(8,128)(2,1)} async-done(((bf16[256,2048]{1,0:T(8,128)(2,1)}), bf16[128,2048]{1,0:T(8,128)(2,1)}) %reduce-scatter.11.cloned.1.call-update) | async-done | bytes 524304 | tf_op jit(solution)/shard_map/reduce_scatter | solution.py:29
  386.4 0.0 copy-done.1
  386.4 2.2 select_subtract_fusion
  (2 shorter events, 0.0 us)
Async XLA Ops:
  7.2 97.9 %all-reduce.3.cloned.1.call-start = ((), (), s32[]{:S(2)}) async-start(), calls=%async_computation.8 | async-start | bytes 2097152 | tf_op jit(solution)/shard_map/psum | solution.py:11
  8.4 126.1 %reduce-scatter.5.cloned.1.call-start = ((), (), s32[]{:S(2)}) async-start(), calls=%async_computation.9 | async-start | bytes 196608 | tf_op jit(solution)/shard_map/reduce_scatter | solution.py:24
  155.9 21.1 %all-to-all-start.1 = ((bf16[128,2,1024]{2,0,1:T(8,128)(2,1)}), bf16[128,2,1024]{2,0,1:T(8,128)(2,1)S(1)}, u32[]{:S(2)}, u32[]{:S(2)}) async-start(bf16[128,2,1024]{2,0,1:T(8,128)(2,1)} %bitcast.49), calls=%async_computation.2 | async-start | bytes 1048576 | tf_op jit(solution)/shard_map/all_to_all | solution.py:26
  159.4 45.2 %reduce-scatter.7.cloned.1.call-start = ((), (), s32[]{:S(2)}) async-start(), calls=%async_computation.10 | async-start | bytes 1572864 | tf_op jit(solution)/shard_map/reduce_scatter | solution.py:29
  177.0 27.5 %copy-start = (f32[128,2048]{1,0:T(8,128)S(1)}, f32[128,2048]{1,0:T(8,128)}, u32[]{:S(2)}) copy-start(f32[128,2048]{1,0:T(8,128)} %param.4) | copy-start | bytes 3145732
  177.0 138.6 %copy-start.2 = (f32[2,128,1024]{2,1,0:T(8,128)S(1)}, f32[2,128,1024]{2,1,0:T(8,128)}, u32[]{:S(2)}) copy-start(f32[2,128,1024]{2,1,0:T(8,128)} %param.5) | copy-start | bytes 3145732
  183.2 117.3 %all-reduce.5.cloned.1.call-start = ((), (), s32[]{:S(2)}) async-start(), calls=%async_computation.11 | async-start | bytes 2097152 | tf_op jit(solution)/shard_map/psum | solution.py:11
  206.8 159.1 %copy-start.3 = (f32[128,128]{1,0:T(8,128)S(1)}, f32[128,128]{1,0:T(8,128)}, u32[]{:S(2)}) copy-start(f32[128,128]{1,0:T(8,128)} %reduce-scatter.5.cloned.1.call-done) | copy-start | bytes 196612
  206.8 179.6 %copy-start.1 = (bf16[128,2048]{1,0:T(8,128)(2,1)S(1)}, bf16[128,2048]{1,0:T(8,128)(2,1)}, u32[]{:S(2)}) copy-start(bf16[128,2048]{1,0:T(8,128)(2,1)} %reduce-scatter.7.cloned.1.call-done) | copy-start | bytes 1572868
  206.8 122.0 %reduce-scatter.9.cloned.1.call-start = ((), (), s32[]{:S(2)}) async-start(), calls=%async_computation.12 | async-start | bytes 196608 | tf_op jit(solution)/shard_map/reduce_scatter | solution.py:24
  317.3 69.1 %reduce-scatter.11.cloned.1.call-start = ((), (), s32[]{:S(2)}) async-start(), calls=%async_computation.13 | async-start | bytes 1572864 | tf_op jit(solution)/shard_map/reduce_scatter | solution.py:29
  328.9 37.0 %copy-start.4 = (f32[128,128]{1,0:T(8,128)S(1)}, f32[128,128]{1,0:T(8,128)}, u32[]{:S(2)}) copy-start(f32[128,128]{1,0:T(8,128)} %reduce-scatter.9.cloned.1.call-done) | copy-start | bytes 196612
Sparse Core Ops, SparseCore 0:
  12.0 92.9 all-reduce.2
  123.1 11.3 reduce-scatter.4
  183.3 21.2 reduce-scatter.6
  208.8 91.5 all-reduce.4
  317.5 11.3 reduce-scatter.8
  366.0 20.3 reduce-scatter.10
where the time goes:
time: 398 us; the launch traced here: 395 us
  waiting for transfers between devices  254 us (64%)
  blocking collectives  80.2 us (20%)
  local copies, waits for them, and re-layouts  20.6 us (5%)
  matrix products  16.3 us (4%)
  between operations  14.2 us (4%)
  other arithmetic  5.94 us (1%)
    psum x2, waiting for transfers between devices, from_root(): return lax.psum(jnp.where(mine, array, jnp.zeros_like(array)), axis)  190 us
    reduce_scatter x2, waiting for transfers between devices, local(): lax.psum_scatter(lax.dot_general(group_cols, panel_now, (((1,), (1,)), ((...  41.2 us
    all_gather x2, blocking collectives, local(): lax.all_gather(own_share.astype(jnp.bfloat16), 'row', axis=1, tiled=True)  39.4 us
    all_to_all x2, blocking collectives, local(): lax.all_to_all(pivot_block, 'blk', split_axis=1, concat_axis=0, tiled=True)  30.5 us
    reduce_scatter x2, waiting for transfers between devices, local(): lax.psum_scatter(partial_value, 'blk', scatter_dimension=0, tiled=True)  23 us
    slice x1, local copies, waits for them, and re-layouts, local(): panel_now = factor_panel[:, section, :]  17.6 us
    dot_general x2, matrix products, local(): lax.dot_general(group_cols, panel_now, (((1,), (1,)), ((), ())), preferre...  12 us
    all_to_all x1, blocking collectives, local(): lax.all_to_all(gathered, 'blk', split_axis=1, concat_axis=0, tiled=True)  10.4 us
  transfers between devices with their start and end apart: 7, of which 6 were waited for; matrix products, arithmetic and copies ran while one was open for 5% of the time, Pallas kernels for 0%

commit v1 on v0

v1 whole, which is shorter than its diff:
```python
import functools

import jax
import jax.numpy as jnp
from jax import lax
from jax.experimental import pallas as pl
from jax.experimental.pallas import tpu as pltpu
from jax.sharding import PartitionSpec as P

MESH = pl.DeviceIdType.MESH
BF16 = jnp.bfloat16
F32 = jnp.float32


def dot_t(a, b):
    return lax.dot_general(a, b, (((1,), (1,)), ((), ())), preferred_element_type=F32)


def kernel(
    n_row, n_blk, cw, cu, cs,
    panel_hbm, right_ref, inverse_ref,
    solved_ref, reduced_ref,
    panel_raw, panel, own_inverse, inverse, side, own_solved, blocks, solved_full, total,
    update_out, update_in,
    panel_sem, inv_send, inv_recv, side_send, side_recv,
    hop_send, hop_recv, line_send, cross_send, core_send, block_recv, upd_send, upd_recv,
):
    row, blk = lax.axis_index("row"), lax.axis_index("blk")
    dates, pixels = right_ref.shape
    steps, width, group = inverse_ref.shape
    chunks = side.shape[1]
    per = n_row // n_blk
    line = n_row // 4
    zz, xx, core = row // 4, lax.rem(row // 2, 2), lax.rem(row, 2)
    chip = row // 2
    cross_row = row + 2 - 4 * xx
    core_row = row + 1 - 2 * core
    my_group = row // per
    my_slot = lax.rem(row, per)
    my_dates = pl.ds(pl.multiple_of(blk * dates, dates), dates)
    n_upd = pixels // cu

    def at_blk(j):
        return lax.rem(blk + j, n_blk)

    def copy_to(src, dst, send, recv, to_row, to_blk):
        return pltpu.make_async_remote_copy(
            src_ref=src, dst_ref=dst, send_sem=send, recv_sem=recv,
            device_id=(to_row, to_blk), device_id_type=MESH,
        )

    load = pltpu.make_async_copy(panel_hbm, panel_raw, panel_sem)
    load.start()

    barrier = pltpu.get_barrier_semaphore()

    def greet(to_row, to_blk):
        pl.semaphore_signal(barrier, inc=1, device_id=(to_row, to_blk), device_id_type=MESH)

    greet(core_row, blk)
    greet(cross_row, blk)
    for d in range(1, line):
        greet(lax.rem(row + 4 * d, n_row), blk)
    for j in range(1, n_blk):
        greet(row, at_blk(j))

    for s in range(steps):
        own_inverse[s] = inverse_ref[s].astype(BF16)

    @pl.when(row == 0)
    def _():
        for i in range(chunks):
            side[0, i] = right_ref[:, i * cw:(i + 1) * cw].astype(BF16)

    pl.semaphore_wait(barrier, 1 + 1 + (line - 1) + (n_blk - 1))

    def inverse_copy(s, j):
        return copy_to(
            own_inverse.at[s], inverse.at[s, blk], inv_send.at[s, j], inv_recv.at[s, blk], row, at_blk(j)
        )

    def inverse_wait(s, j):
        return copy_to(
            own_inverse.at[s], inverse.at[s, at_blk(j)], inv_send.at[s, j], inv_recv.at[s, at_blk(j)],
            row, at_blk(j),
        )

    def side_sends(s, i):
        half = lax.rem(i, 2)
        lane = core == s
        own = xx == half
        ref, recv = side.at[s, i], side_recv.at[s, i]
        down = copy_to(ref, ref, side_send.at[s, i, 0], recv, lax.rem(row + 4, n_row), blk)
        across = copy_to(ref, ref, side_send.at[s, i, 1], recv, cross_row, blk)
        over = copy_to(ref, ref, side_send.at[s, i, 2], recv, core_row, blk)
        return (
            (lane & own & (zz < line - 1), down),
            (lane & ((own & (chip != 1)) | (chip == 0)), across),
            (lane, over),
        )

    def side_start(s, i):
        for need, copy in side_sends(s, i):
            @pl.when(need)
            def _():
                copy.start()

    def side_finish(s):
        def body(i, carry):
            for need, copy in side_sends(s, i):
                @pl.when(need)
                def _():
                    copy.wait_send()
            return carry
        lax.fori_loop(0, chunks, body, 0)

    def side_wait(s, i):
        copy_to(side.at[s, i], side.at[s, i], side_send.at[s, i, 0], side_recv.at[s, i], core_row, blk).wait_recv()

    def split(s, i):
        rows = pl.ds(pl.multiple_of(i * cs, cs), cs)
        pair = panel_raw[rows].reshape(2 * cs, group)
        r = lax.broadcasted_iota(jnp.int32, (cs, 2 * cs), 0)
        c = lax.broadcasted_iota(jnp.int32, (cs, 2 * cs), 1)
        pick = jnp.where(c == 2 * r + s, 1.0, 0.0).astype(BF16)
        panel[s, rows, :] = jnp.dot(pick, pair, preferred_element_type=F32).astype(BF16)

    n_split = pixels // cs // chunks

    def side_stage(s):
        def body(i, carry):
            @pl.when(row != s)
            def _():
                side_wait(s, i)
                side_start(s, i)

            @pl.when(row > s)
            def _():
                @pl.when(i == 0)
                def _():
                    if s == 0:
                        load.wait()
                for m in range(n_split):
                    split(s, i * n_split + m)
            return carry
        lax.fori_loop(0, chunks, body, 0)

    def hop(s):
        return copy_to(
            own_solved.at[s], blocks.at[s, my_slot, my_dates], hop_send.at[s], hop_recv.at[s, blk], row, my_group
        )

    def hop_in(s, j):
        src = at_blk(j)
        where = pl.ds(pl.multiple_of(src * dates, dates), dates)
        return copy_to(
            own_solved.at[s], blocks.at[s, my_slot, where], hop_send.at[s], hop_recv.at[s, src], row, src
        )

    def block_copy(s, slot, send, to_row):
        ref = blocks.at[s, slot]
        return copy_to(ref, ref, send, block_recv.at[s, slot], to_row, blk)

    def line_copy(s, d):
        return block_copy(s, my_slot, line_send.at[s, d], lax.rem(row + 4 * d, n_row))

    def cross_copy(s, slot):
        return block_copy(s, slot, cross_send.at[s, slot], cross_row)

    def core_copy(s, slot):
        return block_copy(s, slot, core_send.at[s, slot], core_row)

    def solve_stage(s):
        for j in range(1, n_blk):
            inverse_wait(s, j).wait_recv()
        inverse[s, blk] = own_inverse[s]
        value = jnp.zeros((dates, width), F32)
        for i in range(chunks):
            at, off = (i * cw) // group, (i * cw) % group
            value = value + dot_t(side[s, i], inverse[s, at, :, off:off + cw])
        solved_ref[s] = value
        half = value.astype(BF16)

        @pl.when(blk != my_group)
        def _():
            own_solved[s] = half
            hop(s).start()

        @pl.when(blk == my_group)
        def _():
            blocks[s, my_slot, my_dates] = half

        if s + 1 < steps:
            for j in range(1, n_blk):
                inverse_copy(s + 1, j).start()

        @pl.when(blk == my_group)
        def _():
            for j in range(1, n_blk):
                hop_in(s, j).wait_recv()
            for d in range(1, line):
                line_copy(s, d).start()
            cross_copy(s, my_slot).start()
            core_copy(s, my_slot).start()

        for turn in range(4):
            x_of = xx if turn % 2 == 0 else 1 - xx
            c_of = core if turn < 2 else 1 - core
            for a in range(per // 4):
                slot = 4 * a + 2 * x_of + c_of
                mine = (blk == my_group) & (slot == my_slot)

                @pl.when(jnp.logical_not(mine))
                def _():
                    block_copy(s, slot, core_send.at[s, slot], core_row).wait_recv()
                    if turn == 0:
                        cross_copy(s, slot).start()
                    if turn < 2:
                        core_copy(s, slot).start()
        solved_full[...] = jnp.concatenate([blocks[s, t] for t in range(per)], axis=1)

    def solve_finish(s):
        @pl.when(blk != my_group)
        def _():
            hop(s).wait_send()

        @pl.when(blk == my_group)
        def _():
            for d in range(1, line):
                line_copy(s, d).wait_send()
        for turn in range(2):
            x_of = xx if turn % 2 == 0 else 1 - xx
            for a in range(per // 4):
                slot = 4 * a + 2 * x_of + core
                if turn == 0:
                    cross_copy(s, slot).wait_send()
                core_copy(s, slot).wait_send()

    def update_copy(i, j):
        return copy_to(
            update_out.at[j, i], update_in.at[blk, i], upd_send.at[j, i], upd_recv.at[blk, i], row, at_blk(j)
        )

    def update_wait(i, j):
        src = at_blk(j)
        return copy_to(
            update_out.at[j, i], update_in.at[src, i], upd_send.at[j, i], upd_recv.at[src, i], row, src
        )

    def pixel_part(i):
        return pl.ds(pl.multiple_of(i * cu, cu), cu)

    def update_out_stage(s, add):
        def body(i, carry):
            cols = pixel_part(i)
            term = dot_t(solved_full[...], panel[s, cols, :])
            if add:
                term = term + total[:, cols]
            total[:, cols] = term
            for j in range(1, n_blk):
                theirs = pl.ds(pl.multiple_of(at_blk(j) * dates, dates), dates)
                update_out[j, i] = total[theirs, cols].astype(BF16)
                update_copy(i, j).start()
            return carry
        lax.fori_loop(0, n_upd, body, 0)

    def reduced_part(i):
        cols = pixel_part(i)
        value = right_ref[:, cols] - total[my_dates, cols]
        for j in range(1, n_blk):
            update_wait(i, j).wait_recv()
            value = value - update_in[at_blk(j), i].astype(F32)
        reduced_ref[:, cols] = value
        return value

    @pl.when(row == 0)
    def _():
        lax.fori_loop(0, chunks, lambda i, c: (side_start(0, i), c)[1], 0)

    for j in range(1, n_blk):
        inverse_copy(0, j).start()

    side_stage(0)
    solve_stage(0)

    @pl.when(row == 0)
    def _():
        load.wait()
        reduced_ref[...] = right_ref[...]

    @pl.when(row == 1)
    def _():
        update_out_stage(0, False)

        def body(i, carry):
            side[1, i] = reduced_part(i).astype(BF16)
            side_start(1, i)
            return carry
        lax.fori_loop(0, n_upd, body, 0)

    @pl.when(row > 1)
    def _():
        def body(i, carry):
            cols = pixel_part(i)
            total[:, cols] = dot_t(solved_full[...], panel[0, cols, :])
            return carry
        lax.fori_loop(0, n_upd, body, 0)

    side_stage(1)
    solve_stage(1)

    @pl.when(row > 1)
    def _():
        update_out_stage(1, True)

        def body(i, carry):
            reduced_part(i)
            return carry
        lax.fori_loop(0, n_upd, body, 0)

    for s in range(steps):
        for j in range(1, n_blk):
            inverse_copy(s, j).wait_send()
        side_finish(s)
        solve_finish(s)

    @pl.when(row > 0)
    def _():
        def body(i, carry):
            for j in range(1, n_blk):
                update_copy(i, j).wait_send()
            return carry
        lax.fori_loop(0, n_upd, body, 0)


def solution(mesh):
    n_row, n_blk = mesh.shape["row"], mesh.shape["blk"]

    def local(factor_panel, right_side, block_inverse):
        pixels, steps, group = factor_panel.shape
        dates = right_side.shape[0]
        width = block_inverse.shape[1]
        order = group * n_blk
        cw = min(256, group)
        chunks = order // cw
        cu, cs = cw, 128
        n_upd = pixels // cu
        per, line = n_row // n_blk, n_row // 4
        dma = pltpu.SemaphoreType.DMA
        return pl.pallas_call(
            functools.partial(kernel, n_row, n_blk, cw, cu, cs),
            out_shape=(
                jax.ShapeDtypeStruct((steps, dates, width), F32),
                jax.ShapeDtypeStruct((dates, pixels), F32),
            ),
            in_specs=[
                pl.BlockSpec(memory_space=pl.ANY),
                pl.BlockSpec(memory_space=pltpu.VMEM),
                pl.BlockSpec(memory_space=pltpu.VMEM),
            ],
            out_specs=(
                pl.BlockSpec(memory_space=pltpu.VMEM),
                pl.BlockSpec(memory_space=pltpu.VMEM),
            ),
            scratch_shapes=[
                pltpu.VMEM((pixels, steps, group), BF16),
                pltpu.VMEM((steps, pixels, group), BF16),
                pltpu.VMEM((steps, width, group), BF16),
                pltpu.VMEM((steps, n_blk, width, group), BF16),
                pltpu.VMEM((steps, chunks, dates, cw), BF16),
                pltpu.VMEM((steps, dates, width), BF16),
                pltpu.VMEM((steps, per, n_blk * dates, width), BF16),
                pltpu.VMEM((n_blk * dates, group), BF16),
                pltpu.VMEM((n_blk * dates, pixels), F32),
                pltpu.VMEM((n_blk, n_upd, dates, cu), BF16),
                pltpu.VMEM((n_blk, n_upd, dates, cu), BF16),
                dma,
                dma((steps, n_blk)),
                dma((steps, n_blk)),
                dma((steps, chunks, 3)),
                dma((steps, chunks)),
                dma((steps,)),
                dma((steps, n_blk)),
                dma((steps, line)),
                dma((steps, per)),
                dma((steps, per)),
                dma((steps, per)),
                dma((n_blk, n_upd)),
                dma((n_blk, n_upd)),
            ],
            compiler_params=pltpu.CompilerParams(
                collective_id=0, has_side_effects=True, vmem_limit_bytes=48 << 20
            ),
        )(factor_panel, right_side, block_inverse)

    return jax.shard_map(
        local,
        mesh=mesh,
        in_specs=(P("row", None, "blk"), P("blk", "row"), P(None, "row", "blk")),
        out_specs=(P(None, "blk", "row"), P("blk", "row")),
        check_vma=False,
    )
```

time: 398 us -> 123 us (0.31)
  waiting for transfers between devices: 254 us -> 0 us
  Pallas kernels: 0 us -> 118 us
  blocking collectives: 80.2 us -> 0 us
  local copies, waits for them, and re-layouts: 20.6 us -> 4.07 us
  matrix products: 16.3 us -> 0 us
  between operations: 14.2 us -> 0.65 us
  other arithmetic: 5.94 us -> 0 us
    psum x2 -> x0, waiting for transfers between devices: 190 us -> none  [from_root(): return lax.psum(jnp.where(mine, array, jnp.zeros_like(array)), axis)]
    pallas_call x0 -> x1, Pallas kernels: none -> 118 us  [local(): pl.pallas_call(functools.partial(kernel, n_row, n_blk, cw, cu, cs), out_s...]
    reduce_scatter x4 -> x0, waiting for transfers between devices: 64.2 us -> none  [the longest x2 41.2 us: local(): lax.psum_scatter(lax.dot_general(group_cols, panel_now, (((1,), (1,)), ((...]
    all_to_all x3 -> x0, blocking collectives: 40.9 us -> none  [the longest x2 30.5 us: local(): lax.all_to_all(pivot_block, 'blk', split_axis=1, concat_axis=0, tiled=True)]
    all_gather x2 -> x0, blocking collectives: 39.4 us -> none  [local(): lax.all_gather(own_share.astype(jnp.bfloat16), 'row', axis=1, tiled=True)]
    slice x1 -> x0, local copies, waits for them, and re-layouts: 17.6 us -> none  [local(): panel_now = factor_panel[:, section, :]]
    dot_general x4 -> x0, matrix products: 16.3 us -> none  [the longest x2 12 us: local(): lax.dot_general(group_cols, panel_now, (((1,), (1,)), ((), ())), preferre...]
    unnamed x10 -> x6, local copies, waits for them, and re-layouts: 0.02 us -> 4.07 us
  transfers between devices with their start and end apart: 7 -> 0, of which waited for: 6 -> 0; matrix products, arithmetic and copies ran while one was open for 5% -> 0% of each run, Pallas kernels for 0% -> 0%
where the time goes in v1:
time: 123 us
  Pallas kernels  118 us (96%)
  local copies, waits for them, and re-layouts  4.07 us (3%)
    pallas_call x1, Pallas kernels, local(): pl.pallas_call(functools.partial(kernel, n_row, n_blk, cw, cu, cs), out_s...  118 us
    unnamed x6, local copies, waits for them, and re-layouts  4.07 us

profile of v1, /device:TPU:3, one launch (start us, length us, event | category | flops | bytes accessed | tf_op | source)
XLA Modules:
  0.0 122.6 jit_solution(15337548589537168786)
XLA Ops:
  0.6 0.0 copy-start
  0.6 1.2 copy-done
  1.9 0.0 copy-start.1
  1.9 1.2 copy-done.1
  3.1 117.9 %shard_map.50 = (f32[2,128,128]{2,1,0:T(8,128)S(1)}, f32[128,2048]{1,0:T(8,128)S(1)}) custom-call(bf16[2048,2,1024]{2,1,0:T(2,128)(2,1)} %panel_hbm.1, f32[128,2048]{1,0:T(8,128)S(1)} %copy-done, f32[2,128,1024]{2,1,0:T(8,128)S(1)} %copy-done.1), custom_call_target="tpu_custom_call" | custom-call | tf_op jit(solution)/shard_map/pallas_call | solution.py:350
  120.9 0.7 copy.7
  121.6 1.0 copy.8
Async XLA Ops:
  0.6 1.2 %copy-start = (f32[128,2048]{1,0:T(8,128)S(1)}, f32[128,2048]{1,0:T(8,128)}, u32[]{:S(2)}) copy-start(f32[128,2048]{1,0:T(8,128)} %right_ref.1) | copy-start | bytes 3145732
  1.9 1.2 copy-start.1

commit v2 on v1

--- a/solution.py
+++ b/solution.py
@@ -74,6 +74,27 @@
 
     pl.semaphore_wait(barrier, 1 + 1 + (line - 1) + (n_blk - 1))
 
+    def holds(j):
+        return j * group < 2 * width * (chip + 1)
+
+    def inverse_start(s):
+        for j in range(1, n_blk):
+            @pl.when(holds(blk))
+            def _():
+                inverse_copy(s, j).start()
+
+    def inverse_finish(s):
+        for j in range(1, n_blk):
+            @pl.when(holds(blk))
+            def _():
+                inverse_copy(s, j).wait_send()
+
+    def inverse_arrive(s):
+        for j in range(1, n_blk):
+            @pl.when(holds(at_blk(j)))
+            def _():
+                inverse_wait(s, j).wait_recv()
+
     def inverse_copy(s, j):
         return copy_to(
             own_inverse.at[s], inverse.at[s, blk], inv_send.at[s, j], inv_recv.at[s, blk], row, at_blk(j)
@@ -84,6 +105,9 @@
             own_inverse.at[s], inverse.at[s, at_blk(j)], inv_send.at[s, j], inv_recv.at[s, at_blk(j)],
             row, at_blk(j),
         )
+
+    def needs(chip_of, i):
+        return i * cw < 2 * width * (chip_of + 1)
 
     def side_sends(s, i):
         half = lax.rem(i, 2)
@@ -93,10 +117,11 @@
         down = copy_to(ref, ref, side_send.at[s, i, 0], recv, lax.rem(row + 4, n_row), blk)
         across = copy_to(ref, ref, side_send.at[s, i, 1], recv, cross_row, blk)
         over = copy_to(ref, ref, side_send.at[s, i, 2], recv, core_row, blk)
+        there = own & (chip != 1) & needs(chip + 1 - 2 * xx, i)
         return (
             (lane & own & (zz < line - 1), down),
-            (lane & ((own & (chip != 1)) | (chip == 0)), across),
-            (lane, over),
+            (lane & (there | ((chip == 0) & jnp.logical_not(own))), across),
+            (lane & needs(chip, i), over),
         )
 
     def side_start(s, i):
@@ -128,22 +153,30 @@
     n_split = pixels // cs // chunks
 
     def side_stage(s):
-        def body(i, carry):
-            @pl.when(row != s)
-            def _():
-                side_wait(s, i)
-                side_start(s, i)
-
-            @pl.when(row > s)
-            def _():
-                @pl.when(i == 0)
+        def turn(own):
+            def body(m, carry):
+                i = 2 * m + (xx if own else 1 - xx)
+                lane = core == s
+                due = needs(chip, i) | (lane if own else False)
+
+                @pl.when((row != s) & due)
                 def _():
-                    if s == 0:
-                        load.wait()
-                for m in range(n_split):
-                    split(s, i * n_split + m)
-            return carry
-        lax.fori_loop(0, chunks, body, 0)
+                    side_wait(s, i)
+                    side_start(s, i)
+
+                @pl.when(row > s)
+                def _():
+                    if s == 0 and own:
+                        @pl.when(m == 0)
+                        def _():
+                            load.wait()
+                    base = (m if own else m + chunks // 2) * n_split
+                    for k in range(n_split):
+                        split(s, base + k)
+                return carry
+            lax.fori_loop(0, chunks // 2, body, 0)
+        turn(True)
+        turn(False)
 
     def hop(s):
         return copy_to(
@@ -171,15 +204,16 @@
         return block_copy(s, slot, core_send.at[s, slot], core_row)
 
     def solve_stage(s):
-        for j in range(1, n_blk):
-            inverse_wait(s, j).wait_recv()
+        inverse_arrive(s)
         inverse[s, blk] = own_inverse[s]
-        value = jnp.zeros((dates, width), F32)
+        solved_ref[s] = jnp.zeros((dates, width), F32)
         for i in range(chunks):
             at, off = (i * cw) // group, (i * cw) % group
-            value = value + dot_t(side[s, i], inverse[s, at, :, off:off + cw])
-        solved_ref[s] = value
-        half = value.astype(BF16)
+
+            @pl.when(needs(chip, i))
+            def _():
+                solved_ref[s] = solved_ref[s] + dot_t(side[s, i], inverse[s, at, :, off:off + cw])
+        half = solved_ref[s].astype(BF16)
 
         @pl.when(blk != my_group)
         def _():
@@ -191,8 +225,7 @@
             blocks[s, my_slot, my_dates] = half
 
         if s + 1 < steps:
-            for j in range(1, n_blk):
-                inverse_copy(s + 1, j).start()
+            inverse_start(s + 1)
 
         @pl.when(blk == my_group)
         def _():
@@ -277,8 +310,7 @@
     def _():
         lax.fori_loop(0, chunks, lambda i, c: (side_start(0, i), c)[1], 0)
 
-    for j in range(1, n_blk):
-        inverse_copy(0, j).start()
+    inverse_start(0)
 
     side_stage(0)
     solve_stage(0)
@@ -319,8 +351,7 @@
         lax.fori_loop(0, n_upd, body, 0)
 
     for s in range(steps):
-        for j in range(1, n_blk):
-            inverse_copy(s, j).wait_send()
+        inverse_finish(s)
         side_finish(s)
         solve_finish(s)
 

time: 123 us -> 88.9 us (0.72)
  the two profiles are of different devices: /device:TPU:3 before, /device:TPU:9 now
where the time goes in v2:
time: 88.9 us; the launch traced here: 88.7 us
  Pallas kernels  84 us (94%)
  local copies, waits for them, and re-layouts  4.07 us (5%)
    pallas_call x1, Pallas kernels, local(): pl.pallas_call(functools.partial(kernel, n_row, n_blk, cw, cu, cs), out_s...  84 us
    unnamed x6, local copies, waits for them, and re-layouts  4.07 us

profile of v2, /device:TPU:9, one launch (start us, length us, event | category | flops | bytes accessed | tf_op | source)
XLA Modules:
  0.0 88.7 jit_solution(4347092211171202632)
XLA Ops:
  0.6 0.0 copy-start
  0.6 1.2 %copy-done = f32[128,2048]{1,0:T(8,128)S(1)} copy-done((f32[128,2048]{1,0:T(8,128)S(1)}, f32[128,2048]{1,0:T(8,128)}, u32[]{:S(2)}) %copy-start) | copy-done | bytes 1048600
  1.9 0.0 copy-start.1
  1.9 1.2 %copy-done.1 = f32[2,128,1024]{2,1,0:T(8,128)S(1)} copy-done((f32[2,128,1024]{2,1,0:T(8,128)S(1)}, f32[2,128,1024]{2,1,0:T(8,128)}, u32[]{:S(2)}) %copy-start.1) | copy-done | bytes 1048600
  3.1 84.0 %shard_map.50 = (f32[2,128,128]{2,1,0:T(8,128)S(1)}, f32[128,2048]{1,0:T(8,128)S(1)}) custom-call(bf16[2048,2,1024]{2,1,0:T(2,128)(2,1)} %panel_hbm.1, f32[128,2048]{1,0:T(8,128)S(1)} %copy-done, f32[2,128,1024]{2,1,0:T(8,128)S(1)} %copy-done.1), custom_call_target="tpu_custom_call" | custom-call | tf_op jit(solution)/shard_map/pallas_call | solution.py:381
  87.1 0.7 copy.7
  87.7 1.0 %copy.8 = f32[128,2048]{1,0:T(8,128)} copy(f32[128,2048]{1,0:T(8,128)S(1)} %get-tuple-element.5) | data formatting | bytes 2097152
Async XLA Ops:
  0.6 1.2 %copy-start = (f32[128,2048]{1,0:T(8,128)S(1)}, f32[128,2048]{1,0:T(8,128)}, u32[]{:S(2)}) copy-start(f32[128,2048]{1,0:T(8,128)} %right_ref.1) | copy-start | bytes 3145732
  1.9 1.2 %copy-start.1 = (f32[2,128,1024]{2,1,0:T(8,128)S(1)}, f32[2,128,1024]{2,1,0:T(8,128)}, u32[]{:S(2)}) copy-start(f32[2,128,1024]{2,1,0:T(8,128)} %inverse_ref.1) | copy-start | bytes 3145732

commit v3 on v2

--- a/solution.py
+++ b/solution.py
@@ -194,8 +194,20 @@
         ref = blocks.at[s, slot]
         return copy_to(ref, ref, send, block_recv.at[s, slot], to_row, blk)
 
-    def line_copy(s, d):
-        return block_copy(s, my_slot, line_send.at[s, d], lax.rem(row + 4 * d, n_row))
+    def line_copies(s, slot):
+        origin = (blk * per + slot) // 4
+        return (
+            ((zz >= origin) & (zz < line - 1),
+             block_copy(s, slot, line_send.at[s, slot, 0], lax.rem(row + 4, n_row))),
+            ((zz <= origin) & (zz > 0),
+             block_copy(s, slot, line_send.at[s, slot, 1], lax.rem(row + n_row - 4, n_row))),
+        )
+
+    def line_start(s, slot):
+        for need, copy in line_copies(s, slot):
+            @pl.when(need)
+            def _():
+                copy.start()
 
     def cross_copy(s, slot):
         return block_copy(s, slot, cross_send.at[s, slot], cross_row)
@@ -231,8 +243,7 @@
         def _():
             for j in range(1, n_blk):
                 hop_in(s, j).wait_recv()
-            for d in range(1, line):
-                line_copy(s, d).start()
+            line_start(s, my_slot)
             cross_copy(s, my_slot).start()
             core_copy(s, my_slot).start()
 
@@ -240,13 +251,15 @@
             x_of = xx if turn % 2 == 0 else 1 - xx
             c_of = core if turn < 2 else 1 - core
             for a in range(per // 4):
-                slot = 4 * a + 2 * x_of + c_of
+                near = jnp.where(zz > blk * (per // 4), per // 4 - 1 - a, a)
+                slot = 4 * near + 2 * x_of + c_of
                 mine = (blk == my_group) & (slot == my_slot)
 
                 @pl.when(jnp.logical_not(mine))
                 def _():
                     block_copy(s, slot, core_send.at[s, slot], core_row).wait_recv()
                     if turn == 0:
+                        line_start(s, slot)
                         cross_copy(s, slot).start()
                     if turn < 2:
                         core_copy(s, slot).start()
@@ -257,15 +270,15 @@
         def _():
             hop(s).wait_send()
 
-        @pl.when(blk == my_group)
-        def _():
-            for d in range(1, line):
-                line_copy(s, d).wait_send()
         for turn in range(2):
             x_of = xx if turn % 2 == 0 else 1 - xx
             for a in range(per // 4):
                 slot = 4 * a + 2 * x_of + core
                 if turn == 0:
+                    for need, copy in line_copies(s, slot):
+                        @pl.when(need)
+                        def _():
+                            copy.wait_send()
                     cross_copy(s, slot).wait_send()
                 core_copy(s, slot).wait_send()
 
@@ -412,7 +425,7 @@
                 dma((steps, chunks)),
                 dma((steps,)),
                 dma((steps, n_blk)),
-                dma((steps, line)),
+                dma((steps, per, 2)),
                 dma((steps, per)),
                 dma((steps, per)),
                 dma((steps, per)),

time: 88.9 us -> 97.9 us (1.10)
  the two profiles are of different devices: /device:TPU:9 before, /device:TPU:3 now
where the time goes in v3:
time: 97.9 us; the launch traced here: 97.8 us
  Pallas kernels  93 us (95%)
  local copies, waits for them, and re-layouts  4.07 us (4%)
    pallas_call x1, Pallas kernels, local(): pl.pallas_call(functools.partial(kernel, n_row, n_blk, cw, cu, cs), out_s...  93 us
    unnamed x6, local copies, waits for them, and re-layouts  4.07 us

profile of v3, /device:TPU:3, one launch (start us, length us, event | category | flops | bytes accessed | tf_op | source)
XLA Modules:
  0.0 97.8 jit_solution(14799059950448417483)
XLA Ops:
  0.6 0.0 copy-start
  0.6 1.2 %copy-done = f32[128,2048]{1,0:T(8,128)S(1)} copy-done((f32[128,2048]{1,0:T(8,128)S(1)}, f32[128,2048]{1,0:T(8,128)}, u32[]{:S(2)}) %copy-start) | copy-done | bytes 1048600
  1.9 0.0 copy-start.1
  1.9 1.2 %copy-done.1 = f32[2,128,1024]{2,1,0:T(8,128)S(1)} copy-done((f32[2,128,1024]{2,1,0:T(8,128)S(1)}, f32[2,128,1024]{2,1,0:T(8,128)}, u32[]{:S(2)}) %copy-start.1) | copy-done | bytes 1048600
  3.1 93.0 %shard_map.50 = (f32[2,128,128]{2,1,0:T(8,128)S(1)}, f32[128,2048]{1,0:T(8,128)S(1)}) custom-call(bf16[2048,2,1024]{2,1,0:T(2,128)(2,1)} %panel_hbm.1, f32[128,2048]{1,0:T(8,128)S(1)} %copy-done, f32[2,128,1024]{2,1,0:T(8,128)S(1)} %copy-done.1), custom_call_target="tpu_custom_call" | custom-call | tf_op jit(solution)/shard_map/pallas_call | solution.py:394
  96.1 0.7 copy.7
  96.8 1.0 copy.8
Async XLA Ops:
  0.6 1.2 %copy-start = (f32[128,2048]{1,0:T(8,128)S(1)}, f32[128,2048]{1,0:T(8,128)}, u32[]{:S(2)}) copy-start(f32[128,2048]{1,0:T(8,128)} %right_ref.1) | copy-start | bytes 3145732
  1.9 1.2 %copy-start.1 = (f32[2,128,1024]{2,1,0:T(8,128)S(1)}, f32[2,128,1024]{2,1,0:T(8,128)}, u32[]{:S(2)}) copy-start(f32[2,128,1024]{2,1,0:T(8,128)} %inverse_ref.1) | copy-start | bytes 3145732
